TPU v7x, 512 devices: a whole 4x8x8 slice. The times are simulated.
512 devices in a mesh: batch: 32 (over x, z), tensor: 16 (over y, core).
Axes of the slice: x: 4, y: 8, z: 8, core: 2. Of those that a mesh axis runs over, the one named last changes fastest.
Arguments:
- queries: bfloat16 [512, 4, 16384], P('batch', None, 'tensor'), may hold values from -8 to 8
- new_kv: bfloat16 [512, 4, 4096], P('batch', None, 'tensor'), may hold values from -6 to 6
- resident_pages: bfloat16 [2688, 64, 4096], P('batch', None, 'tensor'), may hold values from -6 to 6
- arriving_pages: bfloat16 [896, 64, 2048], P('batch', 'tensor'), may hold values from -6 to 6
- block_table: int32 [384, 7], P('batch'), may hold values from 0 to 83, as said below
- old_lengths: int32 [384], P('batch'), may hold values from 1 to 448, as said below
- new_slots: int32 [128], P('batch'), may hold values from 0 to 15, as said below
- page_owner: int32 [896], replicated, may hold values from 0 to 31, as said below
- page_position: int32 [896], replicated, may hold values from 0 to 27, as said below
- page_tokens: int32 [896], replicated, may hold values from 0 to 64, as said below
Outputs:
- attention_out: bfloat16 [512, 4, 16384], P('batch', None, 'tensor')
- arrived_pages: bfloat16 [896, 64, 4096], P('batch', None, 'tensor')
Inputs may be any that keep to these rules, and one draw needn't show every extreme that they name: `block_table`: the rows of one decode group's resident requests name every one of its 84 resident pages exactly once. `old_lengths`: in every decode group one resident request has 448 cached tokens. `new_slots`: within one decode group the slots are distinct and increasing. `page_owner`: every decode group receives exactly 28 arriving pages; one prefill owner sends at most 2 pages to one decode group, and exactly 2 to some. `page_position`: the places of one decode group's arriving pages are distinct; places k * 7 to k * 7 + 6 hold new request k's pages in order. `page_tokens`: A new request of L tokens has min(max(L - i * 64, 0), 64) valid tokens in its page i, and L is at least 1; some new request has 448 tokens.
All inputs are finite; a program needn't handle non-finite values.
Results may differ from a plain program's by a relative error of at most 0.0031.
Values may be sent and summed in bfloat16 or wider, within the bound.
A program may use at most 64 MiB of HBM per device.

v0:
```python
import math

import jax
import jax.numpy as jnp
from jax import lax
from jax.sharding import PartitionSpec as P

HD = 128
KV_HEADS = 8


masked_value = -1e30


def widen_heads(page_data, repeats):
    shaped = page_data.reshape(page_data.shape[:-1] + (KV_HEADS, 2 * HD))
    shaped = jnp.repeat(shaped, repeats, axis=-2)
    return shaped.reshape(page_data.shape[:-1] + (KV_HEADS * repeats * 2 * HD,))


def routing(page_owner, page_position, page_tokens, my_group, sources, per_source, slots_each):
    owners = page_owner.reshape(sources, per_source)
    one_hot = (owners[:, :, None] == jnp.arange(sources, dtype=jnp.int32)[None, None, :]).astype(
        jnp.int32
    )
    page_rank = jnp.sum((jnp.cumsum(one_hot, axis=1) - one_hot) * one_hot, axis=2)
    send_slot = owners * slots_each + page_rank
    arrive_slot = jnp.arange(sources, dtype=jnp.int32)[:, None] * slots_each + page_rank
    target = jnp.where(owners == my_group, page_position.reshape(sources, per_source), per_source)
    chosen = (
        jnp.zeros((per_source,), jnp.int32)
        .at[target.reshape(-1)]
        .set(arrive_slot.reshape(-1), mode="drop")
    )
    counts = (
        jnp.zeros((per_source,), jnp.int32).at[target.reshape(-1)].set(page_tokens, mode="drop")
    )
    return (send_slot, chosen, counts)


def attend(queries, fresh_rows, key_cache, key_valid):
    row_count = queries.shape[0]
    step_count = queries.shape[1]
    copies = key_cache.shape[2] // (2 * HD)
    per_copy = queries.shape[2] // (HD * copies)
    factor = 1.0 / math.sqrt(HD)
    query_view = queries.reshape(row_count, step_count, copies, per_copy, HD)
    query_wide = jnp.concatenate([query_view, jnp.zeros_like(query_view)], axis=-1)
    cache_view = key_cache.reshape(row_count, key_cache.shape[1], copies, 2 * HD)
    fresh_view = fresh_rows.reshape(row_count, step_count, copies, 2 * HD)
    old_scores = (
        jnp.einsum("rsvge,rkve->rsvgk", query_wide, cache_view, preferred_element_type=jnp.float32)
        * factor
    )
    new_scores = (
        jnp.einsum("rsvge,rtve->rsvgt", query_wide, fresh_view, preferred_element_type=jnp.float32)
        * factor
    )
    causal = jnp.arange(step_count)[None, :] <= jnp.arange(step_count)[:, None]
    old_scores = jnp.where(key_valid[:, None, None, None, :], old_scores, masked_value)
    new_scores = jnp.where(causal[None, :, None, None, :], new_scores, masked_value)
    largest = jnp.maximum(jnp.max(old_scores, axis=-1), jnp.max(new_scores, axis=-1))
    old_weights = jnp.exp(old_scores - largest[..., None])
    new_weights = jnp.exp(new_scores - largest[..., None])
    denominator = jnp.sum(old_weights, axis=-1) + jnp.sum(new_weights, axis=-1)
    weighted = jnp.einsum(
        "rsvgk,rkve->rsvge",
        old_weights.astype(jnp.bfloat16),
        cache_view,
        preferred_element_type=jnp.float32,
    )
    weighted = weighted + jnp.einsum(
        "rsvgt,rtve->rsvge",
        new_weights.astype(jnp.bfloat16),
        fresh_view,
        preferred_element_type=jnp.float32,
    )
    result = weighted[..., HD:] / denominator[..., None]
    return result.astype(jnp.bfloat16).reshape(row_count, step_count, copies * per_copy * HD)


def on_device(
    queries,
    new_kv,
    resident_pages,
    arriving_pages,
    block_table,
    old_lengths,
    new_slots,
    page_owner,
    page_position,
    page_tokens,
):
    sources = lax.axis_size("batch")
    my_group = lax.axis_index("batch")
    per_source = arriving_pages.shape[0]
    slots_each = max(2, -(-per_source // sources))
    copies_dev = resident_pages.shape[2] // (2 * HD)
    repeats = copies_dev * lax.axis_size("tensor") // KV_HEADS
    send_slot, chosen, counts = routing(
        page_owner, page_position, page_tokens, my_group, sources, per_source, slots_each
    )
    my_slots = lax.dynamic_index_in_dim(send_slot, my_group, 0, keepdims=False)
    buffer = jnp.zeros((sources * slots_each,) + arriving_pages.shape[1:], arriving_pages.dtype)
    buffer = buffer.at[my_slots].set(arriving_pages)
    moved = lax.all_to_all(buffer, "batch", split_axis=0, concat_axis=0, tiled=True)
    used_rows = moved[chosen]
    arrived = lax.all_to_all(
        widen_heads(used_rows, repeats), "tensor", split_axis=2, concat_axis=1, tiled=True
    )
    request_count = queries.shape[0]
    new_count = new_slots.shape[0]
    old_count = block_table.shape[0]
    pages_each = block_table.shape[1]
    page_size = resident_pages.shape[1]
    width = resident_pages.shape[2]
    new_flag = jnp.zeros((request_count,), jnp.int32).at[new_slots].set(1)
    old_slots = jnp.argsort(new_flag, stable=True)[:old_count]
    key_index = jnp.arange(pages_each * page_size)
    old_valid = key_index[None, :] < old_lengths[:, None]
    page_counts = counts.reshape(new_count, pages_each)
    new_valid = (jnp.arange(page_size)[None, None, :] < page_counts[:, :, None]).reshape(
        new_count, pages_each * page_size
    )
    old_cache = resident_pages[block_table].reshape(old_count, pages_each * page_size, width)
    new_cache = arrived.reshape(new_count, pages_each * page_size, width)
    key_cache = jnp.concatenate([old_cache, new_cache], axis=0)
    key_valid = jnp.concatenate([old_valid, new_valid], axis=0)
    slot_order = jnp.concatenate([old_slots, new_slots])
    result = attend(queries[slot_order], new_kv[slot_order], key_cache, key_valid)
    attention_out = jnp.zeros_like(queries).at[slot_order].set(result)
    return (attention_out, arrived)


def solution(mesh):
    return jax.shard_map(
        on_device,
        mesh=mesh,
        in_specs=(
            P("batch", None, "tensor"),
            P("batch", None, "tensor"),
            P("batch", None, "tensor"),
            P("batch", "tensor", None),
            P("batch", None),
            P("batch"),
            P("batch"),
            P(),
            P(),
            P(),
        ),
        out_specs=(P("batch", None, "tensor"), P("batch", None, "tensor")),
        check_vma=False,
    )
```

profile of v0, /device:TPU:1, one launch (start us, length us, event | category | flops | bytes accessed | tf_op | source)
XLA Modules:
  0.0 137.8 jit_solution(12683812526027921296)
XLA Ops:
  0.7 0.9 reshape.229
  1.7 0.9 fusion.42
  2.8 1.5 %broadcast_in_dim.70 = bf16[64,4,2048]{2,1,0:T(4,128)(2,1)} broadcast(bf16[]{:T(256)} %constant.15.clone.1), dimensions={} | broadcast | bytes 1048578 | tf_op jit(solution)/shard_map/broadcast_in_dim | solution.py:104
  4.4 4.7 %scatter_fusion = bf16[64,4,2048]{2,1,0:T(4,128)(2,1)} fusion(bf16[64,4,2048]{2,1,0:T(4,128)(2,1)} %broadcast_in_dim.70, s32[28]{0:T(128)S(1)} %fusion.31, bf16[28,4,2048]{2,1,0:T(4,128)(2,1)} %param.13), kind=kCustom, calls=%fused_computation.5 | custom fusion | bytes 1376368 | tf_op jit(solution)/shard_map/scatter | solution.py:105
  9.1 13.9 %all-to-all-start = ((bf16[64,4,2048]{2,1,0:T(4,128)(2,1)}), bf16[64,4,2048]{2,1,0:T(4,128)(2,1)}, u32[]{:S(2)}, u32[]{:S(2)}) async-start(bf16[64,4,2048]{2,1,0:T(4,128)(2,1)} %scatter_fusion), calls=%async_computation | async-start | bytes 2097152 | tf_op jit(solution)/shard_map/all_to_all | solution.py:106
  23.2 5.3 %scatter_custom_fusion.2 = s32[28]{0:T(128)S(1)} fusion(s32[896]{0:T(1024)S(1)} %compare_select_fusion, s32[896]{0:T(1024)S(1)} %reshape.289, s32[]{:T(128)} %constant.16.clone.1), kind=kCustom, calls=%fused_computation.67 | custom fusion | bytes 116 | tf_op jit(solution)/shard_map/scatter | solution.py:33
  28.5 19.1 %all-to-all-done = bf16[64,4,2048]{2,1,0:T(4,128)(2,1)} async-done(((bf16[64,4,2048]{2,1,0:T(4,128)(2,1)}), bf16[64,4,2048]{2,1,0:T(4,128)(2,1)}, u32[]{:S(2)}, u32[]{:S(2)}) %all-to-all-start) | async-done | bytes 1048608 | tf_op jit(solution)/shard_map/all_to_all | solution.py:106
  47.6 2.2 %gather_fusion.1 = bf16[28,4,2048]{2,1,0:T(4,128)(2,1)S(1)} fusion(bf16[64,4,2048]{2,1,0:T(4,128)(2,1)} %all-to-all-done, s32[1024]{0:T(1024)S(1)} %pad_clamp_fusion.1), kind=kCustom, calls=%fused_computation.1 | custom fusion | bytes 917616 | tf_op jit(solution)/shard_map/gather | solution.py:107
  49.7 2.7 %copy.33 = bf16[28,4,2048]{0,1,2:T(4,128)(2,1)} copy(bf16[28,4,2048]{2,1,0:T(4,128)(2,1)S(1)} %gather_fusion.1) | data formatting | bytes 917504 | tf_op jit(solution)/shard_map/reshape | solution.py:16
  52.4 5.1 %broadcast_in_dim.74 = bf16[28,4,8,2,256]{0,1,4,3,2:T(4,128)(2,1)} broadcast(bf16[28,4,8,256]{0,1,3,2:T(4,128)(2,1)} %bitcast.80), dimensions={0,1,2,4} | broadcast | bytes 1376256 | tf_op jit(solution)/shard_map/broadcast_in_dim | solution.py:17
  57.6 10.6 %reshape.325 = bf16[16,2,14336]{2,1,0:T(2,128)(2,1)} reshape(bf16[4096,4,28]{2,1,0:T(4,128)(2,1)} %bitcast.78) | data formatting | bytes 1835008
  68.2 12.2 %all-to-all-start.1 = ((bf16[16,2,14336]{2,1,0:T(2,128)(2,1)}), bf16[16,2,14336]{2,1,0:T(2,128)(2,1)}, u32[]{:S(2)}, u32[]{:S(2)}) async-start(bf16[16,2,14336]{2,1,0:T(2,128)(2,1)} %reshape.325), calls=%async_computation.1 | async-start | bytes 1835008 | tf_op jit(solution)/shard_map/all_to_all | solution.py:108
  80.4 5.4 %scatter_custom_fusion.3 = s32[28]{0:T(128)S(1)} fusion(s32[896]{0:T(1024)S(1)} %compare_select_fusion, s32[896]{0:T(1024)} %param.19, s32[]{:T(128)} %constant.16.clone.1), kind=kCustom, calls=%fused_computation.65 | custom fusion | bytes 624 | tf_op jit(solution)/shard_map/scatter | solution.py:36
  86.2 0.8 scatter_custom_fusion
  86.9 1.2 sort.17
  89.8 2.5 %gather_fusion = bf16[84,64,256]{2,1,0:T(8,128)(2,1)} fusion(bf16[84,64,256]{2,1,0:T(8,128)(2,1)S(1)} %copy-done, s32[1024]{0:T(1024)S(1)} %pad_clamp_fusion.2), kind=kCustom, calls=%fused_computation | custom fusion | bytes 5505360 | tf_op jit(solution)/shard_map/gather | solution.py:125
  93.1 12.6 %all-to-all-done.1 = bf16[16,2,14336]{2,1,0:T(2,128)(2,1)} async-done(((bf16[16,2,14336]{2,1,0:T(2,128)(2,1)}), bf16[16,2,14336]{2,1,0:T(2,128)(2,1)}, u32[]{:S(2)}, u32[]{:S(2)}) %all-to-all-start.1) | async-done | bytes 917536 | tf_op jit(solution)/shard_map/all_to_all | solution.py:108
  105.8 13.2 %reshape.326 = bf16[4096,4,28]{2,1,0:T(4,128)(2,1)} reshape(bf16[16,2,14336]{2,1,0:T(2,128)(2,1)} %all-to-all-done.1) | data formatting | bytes 1835008
  119.0 7.2 %copy.30 = bf16[28,4,16,256]{3,1,2,0:T(4,128)(2,1)} copy(bf16[28,4,16,256]{0,1,3,2:T(4,128)(2,1)} %bitcast.79) | data formatting | bytes 1835008 | tf_op jit(solution)/shard_map/all_to_all | solution.py:108
  126.2 2.4 %reshape.231 = bf16[4,448,256]{2,1,0:T(8,128)(2,1)} reshape(bf16[28,16,4,256]{3,2,1,0:T(4,128)(2,1)} %bitcast.81) | data formatting | bytes 1835008 | tf_op jit(solution)/shard_map/reshape | solution.py:126
  128.5 3.4 %fusion.43 = (f32[16,4,8]{2,1,0:T(4,128)S(1)}, f32[16,4,1,8,448]{4,3,1,0,2:T(8,128)S(1)}) fusion(bf16[16,4,1,8,128]{4,3,1,0,2:T(8,128)(2,1)S(1)} %reshape.232, bf16[4,448,256]{2,1,0:T(8,128)(2,1)} %reshape.231, bf16[12,448,256]{2,1,0:T(8,128)(2,1)} %bitcast.83, pred[16,448]{1,0:T(8,128)(4,1)S(1)} %pad_add_fusion), kind=kOutput, calls=%fused_computation.76 | convolution fusion | flops 125468160 | bytes 4727808 | tf_op jit(solution)/shard_map/rsvge,rkve->rsvgk/dot_general | solution.py:52
  132.3 0.8 fusion
  133.1 2.4 %all_to_all.20 = bf16[28,64,256]{2,1,0:T(8,128)(2,1)} reshape(bf16[28,16,4,256]{3,2,1,0:T(4,128)(2,1)} %bitcast.82) | data formatting | bytes 1835008 | tf_op jit(solution)/shard_map/all_to_all | solution.py:108
  136.2 1.0 scatter_fusion.1
  (63 shorter events, 4.9 us)
Async XLA Ops:
  0.6 89.2 %copy-start = (bf16[84,64,256]{2,1,0:T(8,128)(2,1)S(1)}, bf16[84,64,256]{2,1,0:T(8,128)(2,1)}, u32[]{:S(2)}) copy-start(bf16[84,64,256]{2,1,0:T(8,128)(2,1)} %param.12) | copy-start | bytes 8257540
  0.6 22.5 %copy-start.6 = (s32[896]{0:T(1024)S(1)}, s32[896]{0:T(1024)}, u32[]{:S(2)}) copy-start(s32[896]{0:T(1024)} %param.17) | copy-start | bytes 10756
  0.7 22.5 %copy-start.7 = (s32[896]{0:T(1024)S(1)}, s32[896]{0:T(1024)}, u32[]{:S(2)}) copy-start(s32[896]{0:T(1024)} %param.18) | copy-start | bytes 10756
  9.1 38.5 %all-to-all-start = ((bf16[64,4,2048]{2,1,0:T(4,128)(2,1)}), bf16[64,4,2048]{2,1,0:T(4,128)(2,1)}, u32[]{:S(2)}, u32[]{:S(2)}) async-start(bf16[64,4,2048]{2,1,0:T(4,128)(2,1)} %scatter_fusion), calls=%async_computation | async-start | bytes 2097152 | tf_op jit(solution)/shard_map/all_to_all | solution.py:106
  57.5 22.8 %copy-start.10 = (s32[4]{0:T(128)S(1)}, s32[4]{0:T(128)}, u32[]{:S(2)}) copy-start(s32[4]{0:T(128)} %param.16) | copy-start | bytes 52
  57.5 30.7 %copy-start.4 = (bf16[16,4,1024]{2,1,0:T(4,128)(2,1)S(1)}, bf16[16,4,1024]{2,1,0:T(4,128)(2,1)}, u32[]{:S(2)}) copy-start(bf16[16,4,1024]{2,1,0:T(4,128)(2,1)} %param.10) | copy-start | bytes 393220
  57.6 31.5 %copy-start.8 = (s32[12,7]{0,1:T(8,128)S(1)}, s32[12,7]{0,1:T(8,128)}, u32[]{:S(2)}) copy-start(s32[12,7]{0,1:T(8,128)} %param.14) | copy-start | bytes 1012
  57.6 31.7 %copy-start.5 = (bf16[16,4,256]{2,1,0:T(4,128)(2,1)S(1)}, bf16[16,4,256]{2,1,0:T(4,128)(2,1)}, u32[]{:S(2)}) copy-start(bf16[16,4,256]{2,1,0:T(4,128)(2,1)} %param.11) | copy-start | bytes 98308
  68.2 24.2 %copy-start.9 = (s32[12]{0:T(128)S(1)}, s32[12]{0:T(128)}, u32[]{:S(2)}) copy-start(s32[12]{0:T(128)} %param.15) | copy-start | bytes 148
  68.2 37.6 %all-to-all-start.1 = ((bf16[16,2,14336]{2,1,0:T(2,128)(2,1)}), bf16[16,2,14336]{2,1,0:T(2,128)(2,1)}, u32[]{:S(2)}, u32[]{:S(2)}) async-start(bf16[16,2,14336]{2,1,0:T(2,128)(2,1)} %reshape.325), calls=%async_computation.1 | async-start | bytes 1835008 | tf_op jit(solution)/shard_map/all_to_all | solution.py:108
  128.5 3.8 %copy-start.1 = (bf16[84,64,256]{2,1,0:T(8,128)(2,1)S(1)}, bf16[84,64,256]{2,1,0:T(8,128)(2,1)}, u32[]{:S(2)}) copy-start(bf16[84,64,256]{2,1,0:T(8,128)(2,1)} %gather_fusion) | copy-start | bytes 8257540
  128.5 3.8 %copy-start.2 = (bf16[4,448,256]{2,1,0:T(8,128)(2,1)S(1)}, bf16[4,448,256]{2,1,0:T(8,128)(2,1)}, u32[]{:S(2)}) copy-start(bf16[4,448,256]{2,1,0:T(8,128)(2,1)} %reshape.231) | copy-start | bytes 2752516
  137.2 0.7 copy-start.3
where the time goes:
time: 139 us; the launch traced here: 138 us
  local copies, waits for them, and re-layouts  70.7 us (51%)
  waiting for transfers between devices  31.7 us (23%)
  starting transfers between devices  26.1 us (19%)
  matrix products  5.14 us (4%)
  other arithmetic  3.27 us (2%)
    unnamed x24, local copies, waits for them, and re-layouts  24.5 us
    all_to_all x1, waiting for transfers between devices, on_device(): lax.all_to_all(buffer, 'batch', split_axis=0, concat_axis=0, tiled=True)  19.1 us
    all_to_all x1, starting transfers between devices, on_device(): lax.all_to_all(buffer, 'batch', split_axis=0, concat_axis=0, tiled=True)  13.9 us
    all_to_all x1, waiting for transfers between devices, on_device(): lax.all_to_all(widen_heads(used_rows, repeats), 'tensor', split_axis=2, c...  12.6 us
    all_to_all x1, starting transfers between devices, on_device(): lax.all_to_all(widen_heads(used_rows, repeats), 'tensor', split_axis=2, c...  12.2 us
    all_to_all x2, local copies, waits for them, and re-layouts, on_device(): lax.all_to_all(widen_heads(used_rows, repeats), 'tensor', split_axis=2, c...  9.58 us
    scatter x1, local copies, waits for them, and re-layouts, routing(): jnp.zeros((per_source,), jnp.int32).at[target.reshape(-1)]  5.42 us
    scatter x1, local copies, waits for them, and re-layouts, routing(): chosen = jnp.zeros((per_source,), jnp.int32).at[target.reshape(-1)].set(a...  5.26 us
  transfers between devices with their start and end apart: 2, of which 2 were waited for; matrix products, arithmetic and copies ran while one was open for 13% of the time, Pallas kernels for 0%

commit v1 on v0

v1 whole, which is shorter than its diff:
```python
import functools
import math

import jax
import jax.numpy as jnp
from jax import lax
from jax.experimental import pallas as pl
from jax.experimental.pallas import tpu as pltpu
from jax.sharding import PartitionSpec as P

HD = 128
KV_HEADS = 8
MASKED = -1e30
MESH = pl.DeviceIdType.MESH
ANY = pl.BlockSpec(memory_space=pl.ANY)
VMEM = pl.BlockSpec(memory_space=pltpu.VMEM)


def start(copies):
    for copy in copies:
        copy.start()


def wait(copies):
    for copy in copies:
        copy.wait()


def exchange_kernel(
    queries,
    new_kv,
    resident_pages,
    arriving_pages,
    block_table,
    old_lengths,
    new_slots,
    page_owner,
    page_position,
    page_tokens,
    attention_out,
    arrived,
    queries_v,
    new_kv_v,
    resident_v,
    arriving_v,
    table_s,
    lengths_s,
    slots_s,
    owner_s,
    position_s,
    tokens_s,
    send_table_v,
    send_table_s,
    pick_v,
    pick_s,
    key_send,
    key_recv,
    key_turn,
    key_rows,
    value_rows,
    value_send,
    value_recv,
    query_rows,
    fresh_rows,
    result_rows,
    results,
    load_sems,
    table_sems,
    send_sems,
    recv_sems,
):
    groups = lax.axis_size("batch")
    chips = lax.axis_size("tensor") // 2
    me = lax.axis_index("batch")
    place = lax.axis_index("tensor")
    chip = place // 2
    core = place % 2
    half = chip // (chips // 2)
    local = half == core
    pages = arriving_v.shape[0]
    old_count = table_s.shape[0]
    pages_each = table_s.shape[1]
    new_count = slots_s.shape[0]
    request_count = queries_v.shape[0]
    part = KV_HEADS * 4

    barrier = pltpu.get_barrier_semaphore()

    def greet_group(k, carry):
        other = lax.rem(me + k, groups)
        pl.semaphore_signal(barrier, inc=1, device_id=(other, place), device_id_type=MESH)
        return carry

    lax.fori_loop(1, groups, greet_group, 0)

    def greet_place(k, carry):
        other = core * chips + k

        @pl.when(other != place)
        def _():
            pl.semaphore_signal(barrier, inc=1, device_id=(me, other), device_id_type=MESH)

        return carry

    lax.fori_loop(0, chips, greet_place, 0)
    sibling = chip * 2 + 1 - core
    pl.semaphore_signal(barrier, inc=1, device_id=(me, sibling), device_id_type=MESH)

    loads = [
        pltpu.make_async_copy(page_owner, owner_s, load_sems.at[0]),
        pltpu.make_async_copy(arriving_pages, arriving_v, load_sems.at[1]),
        pltpu.make_async_copy(page_position, position_s, load_sems.at[2]),
        pltpu.make_async_copy(page_tokens, tokens_s, load_sems.at[3]),
        pltpu.make_async_copy(block_table, table_s, load_sems.at[4]),
        pltpu.make_async_copy(old_lengths, lengths_s, load_sems.at[5]),
        pltpu.make_async_copy(new_slots, slots_s, load_sems.at[6]),
        pltpu.make_async_copy(queries, queries_v, load_sems.at[7]),
        pltpu.make_async_copy(new_kv, new_kv_v, load_sems.at[8]),
        pltpu.make_async_copy(resident_pages, resident_v, load_sems.at[9]),
    ]
    start(loads)

    row = lax.broadcasted_iota(jnp.int32, (8, 128), 0)
    lane = lax.broadcasted_iota(jnp.int32, (8, 128), 1)
    loads[0].wait()
    first = jnp.zeros((8, 128), jnp.int32)
    last = jnp.zeros((8, 128), jnp.int32)
    for i in range(pages):
        j = pages - 1 - i
        last = jnp.where(lane == owner_s[me * pages + i], i, last)
        first = jnp.where(lane == owner_s[me * pages + j], j, first)
    send_table_v[...] = jnp.where(row == 0, first, last)
    copy = pltpu.make_async_copy(send_table_v, send_table_s, table_sems.at[0])
    copy.start()
    copy.wait()
    loads[1].wait()

    def pack_keys(g, carry):
        for r in range(2):
            page = arriving_v[send_table_s[r, g]]
            for h in range(KV_HEADS):
                key_send[g, r, h] = page[:, 2 * h * HD : (2 * h + 1) * HD]
        return carry

    lax.fori_loop(0, groups, pack_keys, 0)

    pl.semaphore_wait(barrier, groups - 1 + chips + jnp.where(local, 0, 1))

    def to_groups(source, target, n):
        own = pltpu.make_async_copy(source.at[me], target.at[me], recv_sems.at[n])
        own.start()

        def send(k, carry):
            other = lax.rem(me + k, groups)
            pltpu.make_async_remote_copy(
                src_ref=source.at[other],
                dst_ref=target.at[me],
                send_sem=send_sems.at[n],
                recv_sem=recv_sems.at[n],
                device_id=(other, place),
                device_id_type=MESH,
            ).start()
            return carry

        lax.fori_loop(1, groups, send, 0)

    def groups_arrived(target, n):
        pltpu.make_async_copy(target, target, recv_sems.at[n]).wait()

    def groups_sent(source, n):
        part_sent = source.at[pl.ds(0, groups - 1)]
        pltpu.make_async_copy(part_sent, part_sent, send_sems.at[n]).wait()

    def to_chips(source_of, target, n):
        slot = lax.rem(chip, chips // 2) * 2 + core

        @pl.when(local)
        def _():
            pltpu.make_async_copy(source_of(chip), target.at[slot], recv_sems.at[n]).start()

        @pl.when(jnp.logical_not(local))
        def _():
            pltpu.make_async_remote_copy(
                src_ref=source_of(chip),
                dst_ref=target.at[slot],
                send_sem=send_sems.at[n],
                recv_sem=recv_sems.at[n],
                device_id=(me, sibling),
                device_id_type=MESH,
            ).start()

        def send(k, carry):
            other = lax.rem(chip + k, chips)
            pltpu.make_async_remote_copy(
                src_ref=source_of(other),
                dst_ref=target.at[slot],
                send_sem=send_sems.at[n],
                recv_sem=recv_sems.at[n],
                device_id=(me, other * 2 + half),
                device_id_type=MESH,
            ).start()
            return carry

        lax.fori_loop(1, chips, send, 0)

    def chips_arrived(target, n):
        pltpu.make_async_copy(target, target, recv_sems.at[n]).wait()

    def chips_sent(target, n):
        most = target.at[pl.ds(0, chips - 1)]
        pltpu.make_async_copy(most, most, send_sems.at[n]).wait()

        @pl.when(jnp.logical_not(local))
        def _():
            pltpu.make_async_copy(target.at[0], target.at[0], send_sems.at[n]).wait()

    to_groups(key_send, key_recv, 0)
    to_chips(
        lambda h: arriving_v.at[:, :, pl.ds(pl.multiple_of((2 * h + 1) * HD, HD), HD)],
        value_rows,
        1,
    )

    loads[2].wait()
    loads[3].wait()

    def pick(b, carry):
        chosen, counts = carry
        seen = 0
        for i in range(pages):
            j = b * pages + i
            mine = owner_s[j] == me
            hit = lane == jnp.where(mine, position_s[j], -1)
            chosen = jnp.where(hit, 2 * b + seen, chosen)
            counts = jnp.where(hit, tokens_s[j], counts)
            seen = jnp.where(mine, 1, seen)
        return chosen, counts

    zero = jnp.zeros((8, 128), jnp.int32)
    chosen, counts = lax.fori_loop(0, groups, pick, (zero, zero))
    pick_v[...] = jnp.where(row == 0, chosen, counts)
    copy = pltpu.make_async_copy(pick_v, pick_s, table_sems.at[1])
    copy.start()
    copy.wait()
    wait(loads[4:])

    fresh_rows[...] = jnp.zeros_like(fresh_rows)
    factor = 1.0 / math.sqrt(HD)

    def attend(slot, index, cache, length):
        query = queries_v[slot].astype(jnp.float32)
        for g in range(part // 4):
            query_rows[4 * g : 4 * g + 4, :] = query[:, g * HD : (g + 1) * HD]
        fresh_rows[0:4, :] = new_kv_v[slot].astype(jnp.float32)
        fresh = fresh_rows[...].astype(jnp.bfloat16)
        keys = jnp.concatenate([k for k, _ in cache] + [fresh[:, :HD]], axis=0)
        values = jnp.concatenate([v for _, v in cache] + [fresh[:, HD:]], axis=0)
        cached = keys.shape[0] - fresh.shape[0]
        scores = lax.dot_general(
            query_rows[...].astype(jnp.bfloat16),
            keys,
            (((1,), (1,)), ((), ())),
            preferred_element_type=jnp.float32,
        )
        scores = scores * factor
        column = lax.broadcasted_iota(jnp.int32, scores.shape, 1)
        step = lax.rem(lax.broadcasted_iota(jnp.int32, scores.shape, 0), 4)
        bound = jnp.where(column < cached, length, cached + 1 + step)
        scores = jnp.where(column < bound, scores, MASKED)
        largest = jnp.max(scores, axis=1, keepdims=True)
        weights = jnp.exp(scores - largest)
        denominator = jnp.sum(weights, axis=1, keepdims=True)
        weighted = jnp.dot(
            weights.astype(jnp.bfloat16), values, preferred_element_type=jnp.float32
        )
        result_rows[...] = weighted / denominator
        for g in range(part // 4):
            results[index, :, g * HD : (g + 1) * HD] = result_rows[4 * g : 4 * g + 4, :]

    def resident(m, carry):
        slot = m
        for k in range(new_count):
            slot = slot + jnp.where(slots_s[k] <= slot, 1, 0)
        cache = []
        for j in range(pages_each):
            page = resident_v[table_s[m, j]]
            cache.append((page[:, :HD], page[:, HD:]))
        attend(slot, m, cache, lengths_s[m])
        return carry

    lax.fori_loop(0, 4, resident, 0)

    chips_arrived(value_rows, 1)

    def pack_values(g, carry):
        for r in range(2):
            page = value_rows[:, send_table_s[r, g]]
            value_send[g, r] = page.reshape(part, HD)
        return carry

    lax.fori_loop(0, groups, pack_values, 0)
    to_groups(value_send, value_recv, 2)

    lax.fori_loop(4, 6, resident, 0)

    groups_arrived(key_recv, 0)

    def turn_keys(p, carry):
        spot = pick_s[0, p]
        page = key_recv[spot // 2, spot % 2]
        for h in range(KV_HEADS):
            key_turn[h, p] = page[h]
        return carry

    lax.fori_loop(0, pages, turn_keys, 0)
    to_chips(lambda h: key_turn.at[h], key_rows, 3)

    lax.fori_loop(6, old_count, resident, 0)

    chips_arrived(key_rows, 3)
    mine = pl.ds(pl.multiple_of(core * part, part), part)

    def place_keys(p, carry):
        arrived[p, mine, :HD] = key_rows[:, p].reshape(part, HD)
        return carry

    lax.fori_loop(0, pages, place_keys, 0)

    def to_sibling(columns, n):
        return pltpu.make_async_remote_copy(
            src_ref=arrived.at[:, mine, columns],
            dst_ref=arrived.at[:, mine, columns],
            send_sem=send_sems.at[n],
            recv_sem=recv_sems.at[n],
            device_id=(me, sibling),
            device_id_type=MESH,
        )

    key_half = to_sibling(pl.ds(0, HD), 4)
    key_half.start()

    groups_arrived(value_recv, 2)

    def place_values(p, carry):
        spot = pick_s[0, p]
        arrived[p, mine, HD:] = value_recv[spot // 2, spot % 2]
        return carry

    lax.fori_loop(0, pages, place_values, 0)
    value_half = to_sibling(pl.ds(HD, HD), 5)
    value_half.start()
    key_half.wait()
    value_half.wait()

    def fresh_request(k, carry):
        length = 0
        cache = []
        for j in range(pages_each):
            length = length + pick_s[1, k * pages_each + j]
            page = arrived[k * pages_each + j]
            cache.append((page[:, :HD], page[:, HD:]))
        attend(slots_s[k], old_count + k, cache, length)
        return carry

    lax.fori_loop(0, new_count, fresh_request, 0)

    def put(r, carry):
        before = 0
        is_new = 0
        for k in range(new_count):
            before = before + jnp.where(slots_s[k] < r, 1, 0)
            is_new = is_new + jnp.where(slots_s[k] == r, 1, 0)
        index = jnp.where(is_new > 0, old_count + jnp.minimum(before, new_count - 1), jnp.maximum(r - before, 0))
        attention_out[r] = results[index].astype(jnp.bfloat16)
        return carry

    lax.fori_loop(0, request_count, put, 0)

    groups_sent(key_send, 0)
    chips_sent(value_rows, 1)
    groups_sent(value_send, 2)
    chips_sent(key_rows, 3)


def on_device(
    queries,
    new_kv,
    resident_pages,
    arriving_pages,
    block_table,
    old_lengths,
    new_slots,
    page_owner,
    page_position,
    page_tokens,
):
    groups = lax.axis_size("batch")
    pages = arriving_pages.shape[0]
    page_size = resident_pages.shape[1]
    bf16 = jnp.bfloat16
    dma = pltpu.SemaphoreType.DMA
    return pl.pallas_call(
        exchange_kernel,
        name="exchange_and_attend",
        out_shape=(
            jax.ShapeDtypeStruct(queries.shape, queries.dtype),
            jax.ShapeDtypeStruct((pages,) + resident_pages.shape[1:], bf16),
        ),
        in_specs=[ANY] * 10,
        out_specs=(VMEM, VMEM),
        scratch_shapes=[
            pltpu.VMEM(queries.shape, bf16),
            pltpu.VMEM(new_kv.shape, bf16),
            pltpu.VMEM(resident_pages.shape, bf16),
            pltpu.VMEM(arriving_pages.shape, bf16),
            pltpu.SMEM(block_table.shape, jnp.int32),
            pltpu.SMEM(old_lengths.shape, jnp.int32),
            pltpu.SMEM(new_slots.shape, jnp.int32),
            pltpu.SMEM(page_owner.shape, jnp.int32),
            pltpu.SMEM(page_position.shape, jnp.int32),
            pltpu.SMEM(page_tokens.shape, jnp.int32),
            pltpu.VMEM((8, 128), jnp.int32),
            pltpu.SMEM((8, 128), jnp.int32),
            pltpu.VMEM((8, 128), jnp.int32),
            pltpu.SMEM((8, 128), jnp.int32),
            pltpu.VMEM((groups, 2, KV_HEADS, 4, HD), bf16),
            pltpu.VMEM((groups, 2, KV_HEADS, 4, HD), bf16),
            pltpu.VMEM((KV_HEADS, pages, 4, HD), bf16),
            pltpu.VMEM((KV_HEADS, pages, 4, HD), bf16),
            pltpu.VMEM((KV_HEADS, pages, 4, HD), bf16),
            pltpu.VMEM((groups, 2, page_size // 2, HD), bf16),
            pltpu.VMEM((groups, 2, page_size // 2, HD), bf16),
            pltpu.VMEM((page_size // 2, HD), jnp.float32),
            pltpu.VMEM((16, 2 * HD), jnp.float32),
            pltpu.VMEM((page_size // 2, HD), jnp.float32),
            pltpu.VMEM(queries.shape, jnp.float32),
            dma((10,)),
            dma((2,)),
            dma((6,)),
            dma((6,)),
        ],
        compiler_params=pltpu.CompilerParams(
            collective_id=0, has_side_effects=True, vmem_limit_bytes=48 << 20
        ),
    )(
        queries,
        new_kv,
        resident_pages,
        arriving_pages,
        block_table,
        old_lengths,
        new_slots,
        page_owner,
        page_position,
        page_tokens,
    )


def solution(mesh):
    return jax.shard_map(
        on_device,
        mesh=mesh,
        in_specs=(
            P("batch", None, "tensor"),
            P("batch", None, "tensor"),
            P("batch", None, "tensor"),
            P("batch", "tensor", None),
            P("batch", None),
            P("batch"),
            P("batch"),
            P(),
            P(),
            P(),
        ),
        out_specs=(P("batch", None, "tensor"), P("batch", None, "tensor")),
        check_vma=False,
    )
```

time: 139 us -> 55.4 us (0.40)
  the two profiles are of different devices: /device:TPU:1 before, /device:TPU:7 now
where the time goes in v1:
time: 55.4 us; the launch traced here: 54.5 us
  Pallas kernels  43.6 us (79%)
  local copies, waits for them, and re-layouts  10.2 us (18%)
  between operations  0.65 us (1%)
    pallas_call x1, Pallas kernels, on_device(): pl.pallas_call(exchange_kernel, name='exchange_and_attend', out_shape=(ja...  43.6 us
    unnamed x21, local copies, waits for them, and re-layouts  10.2 us

profile of v1, /device:TPU:7, one launch (start us, length us, event | category | flops | bytes accessed | tf_op | source)
XLA Modules:
  0.0 54.5 jit_solution(2745920862039498518)
XLA Ops:
  0.6 0.8 %copy.12.block_table = s32[12,7]{1,0:T(8,128)S(1)} copy(s32[12,7]{0,1:T(8,128)} %param.14) | data formatting | bytes 672 | tf_op args[4]
  1.4 0.0 copy-start
  1.4 1.8 %copy-done = bf16[84,64,256]{2,1,0:T(8,128)(2,1)S(1)} copy-done((bf16[84,64,256]{2,1,0:T(8,128)(2,1)S(1)}, bf16[84,64,256]{2,1,0:T(8,128)(2,1)}, u32[]{:S(2)}) %copy-start) | copy-done | bytes 2752536
  3.2 0.0 copy-start.1
  3.2 1.0 %copy-done.1 = bf16[28,4,2048]{2,1,0:T(4,128)(2,1)S(1)} copy-done((bf16[28,4,2048]{2,1,0:T(4,128)(2,1)S(1)}, bf16[28,4,2048]{2,1,0:T(4,128)(2,1)}, u32[]{:S(2)}) %copy-start.1) | copy-done | bytes 458776
  4.2 0.0 copy-start.2
  4.2 0.9 %copy-done.2 = bf16[16,4,1024]{2,1,0:T(4,128)(2,1)S(1)} copy-done((bf16[16,4,1024]{2,1,0:T(4,128)(2,1)S(1)}, bf16[16,4,1024]{2,1,0:T(4,128)(2,1)}, u32[]{:S(2)}) %copy-start.2) | copy-done | bytes 131096
  5.1 0.0 copy-start.3
  5.1 0.8 %copy-done.3 = bf16[16,4,256]{2,1,0:T(4,128)(2,1)S(1)} copy-done((bf16[16,4,256]{2,1,0:T(4,128)(2,1)S(1)}, bf16[16,4,256]{2,1,0:T(4,128)(2,1)}, u32[]{:S(2)}) %copy-start.3) | copy-done | bytes 32792
  5.9 0.0 copy-start.4
  5.9 0.7 %copy-done.4 = s32[896]{0:T(1024)S(1)} copy-done((s32[896]{0:T(1024)S(1)}, s32[896]{0:T(1024)}, u32[]{:S(2)}) %copy-start.4) | copy-done | bytes 3608
  6.6 0.0 copy-start.5
  6.6 0.7 %copy-done.5 = s32[896]{0:T(1024)S(1)} copy-done((s32[896]{0:T(1024)S(1)}, s32[896]{0:T(1024)}, u32[]{:S(2)}) %copy-start.5) | copy-done | bytes 3608
  7.2 0.0 copy-start.6
  7.2 0.7 %copy-done.6 = s32[896]{0:T(1024)S(1)} copy-done((s32[896]{0:T(1024)S(1)}, s32[896]{0:T(1024)}, u32[]{:S(2)}) %copy-start.6) | copy-done | bytes 3608
  7.9 0.0 copy-start.7
  7.9 0.7 %copy-done.7 = s32[12]{0:T(128)S(1)} copy-done((s32[12]{0:T(128)S(1)}, s32[12]{0:T(128)}, u32[]{:S(2)}) %copy-start.7) | copy-done | bytes 72
  8.6 0.0 copy-start.8
  8.6 0.7 %copy-done.8 = s32[4]{0:T(128)S(1)} copy-done((s32[4]{0:T(128)S(1)}, s32[4]{0:T(128)}, u32[]{:S(2)}) %copy-start.8) | copy-done | bytes 40
  9.2 43.6 %exchange_and_attend.1 = (bf16[16,4,1024]{2,1,0:T(4,128)(2,1)S(1)}, bf16[28,64,256]{2,1,0:T(8,128)(2,1)S(1)}) custom-call(bf16[16,4,1024]{2,1,0:T(4,128)(2,1)S(1)} %copy-done.2, bf16[16,4,256]{2,1,0:T(4,128)(2,1)S(1)} %copy-done.3, bf16[84,64,256]{2,1,0:T(8,128)(2,1)S(1)} %copy-done, bf16[28,4,2048]{2,1,0:T(4,128)(2,1)S(1)} %copy-done.1, ...), custom_call_target="tpu_custom_call" | custom-call | tf_op jit(solution)/shard_map/exchange_and_attend/pallas_call | solution.py:402
  52.9 0.7 %copy.15 = bf16[16,4,1024]{2,1,0:T(4,128)(2,1)} copy(bf16[16,4,1024]{2,1,0:T(4,128)(2,1)S(1)} %get-tuple-element.4) | data formatting | bytes 262144
  53.5 0.9 %copy.16 = bf16[28,64,256]{2,1,0:T(8,128)(2,1)} copy(bf16[28,64,256]{2,1,0:T(8,128)(2,1)S(1)} %get-tuple-element.5) | data formatting | bytes 1835008
Async XLA Ops:
  1.4 1.8 %copy-start = (bf16[84,64,256]{2,1,0:T(8,128)(2,1)S(1)}, bf16[84,64,256]{2,1,0:T(8,128)(2,1)}, u32[]{:S(2)}) copy-start(bf16[84,64,256]{2,1,0:T(8,128)(2,1)} %resident_pages.1) | copy-start | bytes 8257540
  3.2 1.0 %copy-start.1 = (bf16[28,4,2048]{2,1,0:T(4,128)(2,1)S(1)}, bf16[28,4,2048]{2,1,0:T(4,128)(2,1)}, u32[]{:S(2)}) copy-start(bf16[28,4,2048]{2,1,0:T(4,128)(2,1)} %arriving_pages.1) | copy-start | bytes 1376260
  4.2 0.9 %copy-start.2 = (bf16[16,4,1024]{2,1,0:T(4,128)(2,1)S(1)}, bf16[16,4,1024]{2,1,0:T(4,128)(2,1)}, u32[]{:S(2)}) copy-start(bf16[16,4,1024]{2,1,0:T(4,128)(2,1)} %queries.1) | copy-start | bytes 393220
  5.1 0.8 %copy-start.3 = (bf16[16,4,256]{2,1,0:T(4,128)(2,1)S(1)}, bf16[16,4,256]{2,1,0:T(4,128)(2,1)}, u32[]{:S(2)}) copy-start(bf16[16,4,256]{2,1,0:T(4,128)(2,1)} %new_kv.1) | copy-start | bytes 98308
  5.9 0.7 %copy-start.4 = (s32[896]{0:T(1024)S(1)}, s32[896]{0:T(1024)}, u32[]{:S(2)}) copy-start(s32[896]{0:T(1024)} %page_owner.1) | copy-start | bytes 10756
  6.6 0.7 %copy-start.5 = (s32[896]{0:T(1024)S(1)}, s32[896]{0:T(1024)}, u32[]{:S(2)}) copy-start(s32[896]{0:T(1024)} %page_position.1) | copy-start | bytes 10756
  7.2 0.7 %copy-start.6 = (s32[896]{0:T(1024)S(1)}, s32[896]{0:T(1024)}, u32[]{:S(2)}) copy-start(s32[896]{0:T(1024)} %page_tokens.1) | copy-start | bytes 10756
  7.9 0.7 %copy-start.7 = (s32[12]{0:T(128)S(1)}, s32[12]{0:T(128)}, u32[]{:S(2)}) copy-start(s32[12]{0:T(128)} %old_lengths.1) | copy-start | bytes 148
  8.6 0.7 %copy-start.8 = (s32[4]{0:T(128)S(1)}, s32[4]{0:T(128)}, u32[]{:S(2)}) copy-start(s32[4]{0:T(128)} %new_slots.1) | copy-start | bytes 52

commit v2 on v1

--- a/solution.py
+++ b/solution.py
@@ -78,8 +78,8 @@
     half = chip // (chips // 2)
     local = half == core
     pages = arriving_v.shape[0]
-    old_count = table_s.shape[0]
-    pages_each = table_s.shape[1]
+    old_count = table_s.shape[1]
+    pages_each = table_s.shape[0]
     new_count = slots_s.shape[0]
     request_count = queries_v.shape[0]
     part = KV_HEADS * 4
@@ -283,7 +283,7 @@
             slot = slot + jnp.where(slots_s[k] <= slot, 1, 0)
         cache = []
         for j in range(pages_each):
-            page = resident_v[table_s[m, j]]
+            page = resident_v[table_s[j, m]]
             cache.append((page[:, :HD], page[:, HD:]))
         attend(slot, m, cache, lengths_s[m])
         return carry
@@ -413,7 +413,7 @@
             pltpu.VMEM(new_kv.shape, bf16),
             pltpu.VMEM(resident_pages.shape, bf16),
             pltpu.VMEM(arriving_pages.shape, bf16),
-            pltpu.SMEM(block_table.shape, jnp.int32),
+            pltpu.SMEM(block_table.shape[::-1], jnp.int32),
             pltpu.SMEM(old_lengths.shape, jnp.int32),
             pltpu.SMEM(new_slots.shape, jnp.int32),
             pltpu.SMEM(page_owner.shape, jnp.int32),
@@ -443,16 +443,21 @@
             collective_id=0, has_side_effects=True, vmem_limit_bytes=48 << 20
         ),
     )(
-        queries,
-        new_kv,
-        resident_pages,
-        arriving_pages,
-        block_table,
-        old_lengths,
-        new_slots,
-        page_owner,
-        page_position,
-        page_tokens,
+        *(
+            pltpu.with_memory_space_constraint(x, pltpu.HBM)
+            for x in (
+                queries,
+                new_kv,
+                resident_pages,
+                arriving_pages,
+                block_table.T,
+                old_lengths,
+                new_slots,
+                page_owner,
+                page_position,
+                page_tokens,
+            )
+        )
     )
 
 

time: 55.4 us -> 46.5 us (0.84)
  local copies, waits for them, and re-layouts: 10.2 us -> 1.58 us
    unnamed x21 -> x2, local copies, waits for them, and re-layouts: 10.2 us -> 1.58 us
where the time goes in v2:
time: 46.5 us; the launch traced here: 45.9 us
  Pallas kernels  43.6 us (94%)
  local copies, waits for them, and re-layouts  1.58 us (3%)
  between operations  0.64 us (1%)
    pallas_call x1, Pallas kernels, on_device(): pl.pallas_call(exchange_kernel, name='exchange_and_attend', out_shape=(ja...  43.6 us
    unnamed x2, local copies, waits for them, and re-layouts  1.58 us

profile of v2, /device:TPU:7, one launch (start us, length us, event | category | flops | bytes accessed | tf_op | source)
XLA Modules:
  0.0 45.9 jit_solution(12138245037748087445)
XLA Ops:
  0.6 43.6 %exchange_and_attend.1 = (bf16[16,4,1024]{2,1,0:T(4,128)(2,1)S(1)}, bf16[28,64,256]{2,1,0:T(8,128)(2,1)S(1)}) custom-call(bf16[16,4,1024]{2,1,0:T(4,128)(2,1)} %queries.1, bf16[16,4,256]{2,1,0:T(4,128)(2,1)} %new_kv.1, bf16[84,64,256]{2,1,0:T(8,128)(2,1)} %resident_pages.1, bf16[28,4,2048]{2,1,0:T(4,128)(2,1)} %arriving_pages.1, s32[7,12]{1,0:T(8,128)} %bitcast.1, ...), custom_call_target="tpu_custom_call" | custom-call | tf_op jit(solution)/shard_map/exchange_and_attend/pallas_call | solution.py:402
  44.3 0.7 %copy.14 = bf16[16,4,1024]{2,1,0:T(4,128)(2,1)} copy(bf16[16,4,1024]{2,1,0:T(4,128)(2,1)S(1)} %get-tuple-element.4) | data formatting | bytes 262144
  44.9 0.9 %copy.15 = bf16[28,64,256]{2,1,0:T(8,128)(2,1)} copy(bf16[28,64,256]{2,1,0:T(8,128)(2,1)S(1)} %get-tuple-element.5) | data formatting | bytes 1835008

commit v3 on v2

--- a/solution.py
+++ b/solution.py
@@ -24,6 +24,52 @@
 def wait(copies):
     for copy in copies:
         copy.wait()
+
+
+def split_rows(rows, staging, target, index):
+    staging[...] = rows
+    for g in range(rows.shape[0] // 4):
+        piece = staging[4 * g : 4 * g + 4, :].astype(jnp.bfloat16)
+        target[index, :, g * HD : (g + 1) * HD] = piece
+
+
+def finish_kernel(
+    arrived,
+    results,
+    fresh_weights,
+    fresh_sums,
+    denominators,
+    new_slots,
+    attention_out,
+    arrived_out,
+    slots_s,
+    rows_v,
+    sems,
+):
+    slots_copy = pltpu.make_async_copy(new_slots, slots_s, sems.at[0])
+    slots_copy.start()
+    copy = pltpu.make_async_copy(arrived, arrived_out, sems.at[1])
+    copy.start()
+    other = 1 - lax.axis_index("tensor") % 2
+    part = rows_v.shape[0]
+    others = pl.ds(pl.multiple_of(other * part, part), part)
+    new_count = fresh_sums.shape[0]
+    pages_each = arrived.shape[0] // new_count
+    slots_copy.wait()
+    for m in range(results.shape[0]):
+        slot = m
+        for k in range(new_count):
+            slot = slot + jnp.where(slots_s[k] <= slot, 1, 0)
+        attention_out[slot] = results[m]
+    for k in range(new_count):
+        first_page = k * pages_each
+        values = jnp.concatenate(
+            [arrived[first_page + j, others, HD:] for j in range(pages_each)], axis=0
+        )
+        rows = jnp.dot(fresh_weights[k, other], values, preferred_element_type=jnp.float32)
+        rows = (fresh_sums[k] + rows) / denominators[k]
+        split_rows(rows, rows_v, attention_out, slots_s[k])
+    copy.wait()
 
 
 def exchange_kernel(
@@ -37,8 +83,11 @@
     page_owner,
     page_position,
     page_tokens,
-    attention_out,
     arrived,
+    results,
+    fresh_weights,
+    fresh_sums,
+    denominators,
     queries_v,
     new_kv_v,
     resident_v,
@@ -63,7 +112,6 @@
     query_rows,
     fresh_rows,
     result_rows,
-    results,
     load_sems,
     table_sems,
     send_sems,
@@ -81,30 +129,8 @@
     old_count = table_s.shape[1]
     pages_each = table_s.shape[0]
     new_count = slots_s.shape[0]
-    request_count = queries_v.shape[0]
+    page_size = arrived.shape[1]
     part = KV_HEADS * 4
-
-    barrier = pltpu.get_barrier_semaphore()
-
-    def greet_group(k, carry):
-        other = lax.rem(me + k, groups)
-        pl.semaphore_signal(barrier, inc=1, device_id=(other, place), device_id_type=MESH)
-        return carry
-
-    lax.fori_loop(1, groups, greet_group, 0)
-
-    def greet_place(k, carry):
-        other = core * chips + k
-
-        @pl.when(other != place)
-        def _():
-            pl.semaphore_signal(barrier, inc=1, device_id=(me, other), device_id_type=MESH)
-
-        return carry
-
-    lax.fori_loop(0, chips, greet_place, 0)
-    sibling = chip * 2 + 1 - core
-    pl.semaphore_signal(barrier, inc=1, device_id=(me, sibling), device_id_type=MESH)
 
     loads = [
         pltpu.make_async_copy(page_owner, owner_s, load_sems.at[0]),
@@ -118,7 +144,32 @@
         pltpu.make_async_copy(new_kv, new_kv_v, load_sems.at[8]),
         pltpu.make_async_copy(resident_pages, resident_v, load_sems.at[9]),
     ]
-    start(loads)
+    start(loads[:2])
+
+    barrier = pltpu.get_barrier_semaphore()
+
+    def peer(k):
+        return jnp.where(k < me, k, k + 1)
+
+    def greet_group(k, carry):
+        pl.semaphore_signal(barrier, inc=1, device_id=(peer(k), place), device_id_type=MESH)
+        return carry
+
+    lax.fori_loop(0, groups - 1, greet_group, 0)
+
+    def greet_place(k, carry):
+        other = core * chips + k
+
+        @pl.when(other != place)
+        def _():
+            pl.semaphore_signal(barrier, inc=1, device_id=(me, other), device_id_type=MESH)
+
+        return carry
+
+    lax.fori_loop(0, chips, greet_place, 0)
+    sibling = chip * 2 + 1 - core
+    pl.semaphore_signal(barrier, inc=1, device_id=(me, sibling), device_id_type=MESH)
+    start(loads[2:])
 
     row = lax.broadcasted_iota(jnp.int32, (8, 128), 0)
     lane = lax.broadcasted_iota(jnp.int32, (8, 128), 1)
@@ -137,12 +188,12 @@
 
     def pack_keys(g, carry):
         for r in range(2):
-            page = arriving_v[send_table_s[r, g]]
+            page = send_table_s[r, g]
             for h in range(KV_HEADS):
-                key_send[g, r, h] = page[:, 2 * h * HD : (2 * h + 1) * HD]
-        return carry
-
-    lax.fori_loop(0, groups, pack_keys, 0)
+                key_send[g, r, h] = arriving_v[page, :, 2 * h * HD : (2 * h + 1) * HD]
+        return carry
+
+    lax.fori_loop(0, groups, pack_keys, 0, unroll=4)
 
     pl.semaphore_wait(barrier, groups - 1 + chips + jnp.where(local, 0, 1))
 
@@ -151,7 +202,7 @@
         own.start()
 
         def send(k, carry):
-            other = lax.rem(me + k, groups)
+            other = peer(k)
             pltpu.make_async_remote_copy(
                 src_ref=source.at[other],
                 dst_ref=target.at[me],
@@ -162,7 +213,7 @@
             ).start()
             return carry
 
-        lax.fori_loop(1, groups, send, 0)
+        lax.fori_loop(0, groups - 1, send, 0)
 
     def groups_arrived(target, n):
         pltpu.make_async_copy(target, target, recv_sems.at[n]).wait()
@@ -221,6 +272,67 @@
         1,
     )
 
+    wait(loads[4:])
+
+    fresh_rows[...] = jnp.zeros_like(fresh_rows)
+    factor = 1.0 / math.sqrt(HD)
+
+    def read_query(slot):
+        query = queries_v[slot].astype(jnp.float32)
+        for g in range(part // 4):
+            query_rows[4 * g : 4 * g + 4, :] = query[:, g * HD : (g + 1) * HD]
+        fresh_rows[0:4, :] = new_kv_v[slot].astype(jnp.float32)
+        return query_rows[...].astype(jnp.bfloat16), fresh_rows[...].astype(jnp.bfloat16)
+
+    def score(query, keys):
+        return factor * lax.dot_general(
+            query, keys, (((1,), (1,)), ((), ())), preferred_element_type=jnp.float32
+        )
+
+    def weigh(weights, values):
+        return jnp.dot(weights.astype(jnp.bfloat16), values, preferred_element_type=jnp.float32)
+
+    def store_result(index, rows):
+        split_rows(rows, result_rows, results, index)
+
+    def columns_of(scores):
+        return lax.broadcasted_iota(jnp.int32, scores.shape, 1)
+
+    def rows_of(scores):
+        return lax.broadcasted_iota(jnp.int32, scores.shape, 0)
+
+    def resident(m, carry):
+        slot = m
+        for k in range(new_count):
+            slot = slot + jnp.where(slots_s[k] <= slot, 1, 0)
+        query, fresh = read_query(slot)
+        pages_read = [resident_v[table_s[j, m]] for j in range(pages_each)]
+        cache = jnp.concatenate(pages_read + [fresh], axis=0)
+        scores = score(query, cache[:, :HD])
+        column = columns_of(scores)
+        step = lax.rem(rows_of(scores), 4)
+        cached = pages_each * page_size
+        bound = jnp.where(column < cached, lengths_s[m], cached + 1 + step)
+        scores = jnp.where(column < bound, scores, MASKED)
+        largest = jnp.max(scores, axis=1, keepdims=True)
+        weights = jnp.exp(scores - largest)
+        denominator = jnp.sum(weights, axis=1, keepdims=True)
+        store_result(m, weigh(weights, cache[:, HD:]) / denominator)
+        return carry
+
+    lax.fori_loop(0, 3, resident, 0)
+
+    chips_arrived(value_rows, 1)
+
+    def pack_values(g, carry):
+        for r in range(2):
+            page = value_rows[:, send_table_s[r, g]]
+            value_send[g, r] = page.reshape(part, HD)
+        return carry
+
+    lax.fori_loop(0, groups, pack_values, 0, unroll=2)
+    to_groups(value_send, value_recv, 2)
+
     loads[2].wait()
     loads[3].wait()
 
@@ -242,66 +354,7 @@
     copy = pltpu.make_async_copy(pick_v, pick_s, table_sems.at[1])
     copy.start()
     copy.wait()
-    wait(loads[4:])
-
-    fresh_rows[...] = jnp.zeros_like(fresh_rows)
-    factor = 1.0 / math.sqrt(HD)
-
-    def attend(slot, index, cache, length):
-        query = queries_v[slot].astype(jnp.float32)
-        for g in range(part // 4):
-            query_rows[4 * g : 4 * g + 4, :] = query[:, g * HD : (g + 1) * HD]
-        fresh_rows[0:4, :] = new_kv_v[slot].astype(jnp.float32)
-        fresh = fresh_rows[...].astype(jnp.bfloat16)
-        keys = jnp.concatenate([k for k, _ in cache] + [fresh[:, :HD]], axis=0)
-        values = jnp.concatenate([v for _, v in cache] + [fresh[:, HD:]], axis=0)
-        cached = keys.shape[0] - fresh.shape[0]
-        scores = lax.dot_general(
-            query_rows[...].astype(jnp.bfloat16),
-            keys,
-            (((1,), (1,)), ((), ())),
-            preferred_element_type=jnp.float32,
-        )
-        scores = scores * factor
-        column = lax.broadcasted_iota(jnp.int32, scores.shape, 1)
-        step = lax.rem(lax.broadcasted_iota(jnp.int32, scores.shape, 0), 4)
-        bound = jnp.where(column < cached, length, cached + 1 + step)
-        scores = jnp.where(column < bound, scores, MASKED)
-        largest = jnp.max(scores, axis=1, keepdims=True)
-        weights = jnp.exp(scores - largest)
-        denominator = jnp.sum(weights, axis=1, keepdims=True)
-        weighted = jnp.dot(
-            weights.astype(jnp.bfloat16), values, preferred_element_type=jnp.float32
-        )
-        result_rows[...] = weighted / denominator
-        for g in range(part // 4):
-            results[index, :, g * HD : (g + 1) * HD] = result_rows[4 * g : 4 * g + 4, :]
-
-    def resident(m, carry):
-        slot = m
-        for k in range(new_count):
-            slot = slot + jnp.where(slots_s[k] <= slot, 1, 0)
-        cache = []
-        for j in range(pages_each):
-            page = resident_v[table_s[j, m]]
-            cache.append((page[:, :HD], page[:, HD:]))
-        attend(slot, m, cache, lengths_s[m])
-        return carry
-
-    lax.fori_loop(0, 4, resident, 0)
-
-    chips_arrived(value_rows, 1)
-
-    def pack_values(g, carry):
-        for r in range(2):
-            page = value_rows[:, send_table_s[r, g]]
-            value_send[g, r] = page.reshape(part, HD)
-        return carry
-
-    lax.fori_loop(0, groups, pack_values, 0)
-    to_groups(value_send, value_recv, 2)
-
-    lax.fori_loop(4, 6, resident, 0)
+    lax.fori_loop(3, 7, resident, 0)
 
     groups_arrived(key_recv, 0)
 
@@ -312,10 +365,10 @@
             key_turn[h, p] = page[h]
         return carry
 
-    lax.fori_loop(0, pages, turn_keys, 0)
+    lax.fori_loop(0, pages, turn_keys, 0, unroll=4)
     to_chips(lambda h: key_turn.at[h], key_rows, 3)
 
-    lax.fori_loop(6, old_count, resident, 0)
+    lax.fori_loop(7, old_count, resident, 0)
 
     chips_arrived(key_rows, 3)
     mine = pl.ds(pl.multiple_of(core * part, part), part)
@@ -324,7 +377,7 @@
         arrived[p, mine, :HD] = key_rows[:, p].reshape(part, HD)
         return carry
 
-    lax.fori_loop(0, pages, place_keys, 0)
+    lax.fori_loop(0, pages, place_keys, 0, unroll=4)
 
     def to_sibling(columns, n):
         return pltpu.make_async_remote_copy(
@@ -339,6 +392,41 @@
     key_half = to_sibling(pl.ds(0, HD), 4)
     key_half.start()
 
+    key_half.wait()
+
+    def half_of(k, rows, columns):
+        first_page = k * pages_each
+        return jnp.concatenate(
+            [arrived[first_page + j, rows, columns] for j in range(pages_each)], axis=0
+        )
+
+    def fresh_scores(k, carry):
+        length = 0
+        for j in range(pages_each):
+            length = length + pick_s[1, k * pages_each + j]
+        query, fresh = read_query(slots_s[k])
+        scores = []
+        for c in range(2):
+            keys = half_of(k, pl.ds(c * part, part), pl.ds(0, HD))
+            cached = score(query, keys)
+            column = columns_of(cached)
+            position = column // part * page_size + c * part + column % part
+            scores.append(jnp.where(position < length, cached, MASKED))
+        own = score(query, fresh[:, :HD])
+        scores.append(jnp.where(columns_of(own) <= lax.rem(rows_of(own), 4), own, MASKED))
+        largest = functools.reduce(
+            jnp.maximum, [jnp.max(x, axis=1, keepdims=True) for x in scores]
+        )
+        weights = [jnp.exp(x - largest) for x in scores]
+        denominator = sum(jnp.sum(x, axis=1, keepdims=True) for x in weights)
+        for c in range(2):
+            fresh_weights[k, c] = weights[c].astype(jnp.bfloat16)
+        fresh_sums[k] = weigh(weights[2], fresh[:, HD:])
+        denominators[k] = jnp.broadcast_to(denominator, denominators.shape[1:])
+        return carry
+
+    lax.fori_loop(0, new_count, fresh_scores, 0)
+
     groups_arrived(value_recv, 2)
 
     def place_values(p, carry):
@@ -346,35 +434,14 @@
         arrived[p, mine, HD:] = value_recv[spot // 2, spot % 2]
         return carry
 
-    lax.fori_loop(0, pages, place_values, 0)
+    lax.fori_loop(0, pages, place_values, 0, unroll=7)
     value_half = to_sibling(pl.ds(HD, HD), 5)
     value_half.start()
-    key_half.wait()
+
+    for k in range(new_count):
+        fresh_sums[k] += weigh(fresh_weights[k, core], half_of(k, mine, pl.ds(HD, HD)))
+
     value_half.wait()
-
-    def fresh_request(k, carry):
-        length = 0
-        cache = []
-        for j in range(pages_each):
-            length = length + pick_s[1, k * pages_each + j]
-            page = arrived[k * pages_each + j]
-            cache.append((page[:, :HD], page[:, HD:]))
-        attend(slots_s[k], old_count + k, cache, length)
-        return carry
-
-    lax.fori_loop(0, new_count, fresh_request, 0)
-
-    def put(r, carry):
-        before = 0
-        is_new = 0
-        for k in range(new_count):
-            before = before + jnp.where(slots_s[k] < r, 1, 0)
-            is_new = is_new + jnp.where(slots_s[k] == r, 1, 0)
-        index = jnp.where(is_new > 0, old_count + jnp.minimum(before, new_count - 1), jnp.maximum(r - before, 0))
-        attention_out[r] = results[index].astype(jnp.bfloat16)
-        return carry
-
-    lax.fori_loop(0, request_count, put, 0)
 
     groups_sent(key_send, 0)
     chips_sent(value_rows, 1)
@@ -397,17 +464,23 @@
     groups = lax.axis_size("batch")
     pages = arriving_pages.shape[0]
     page_size = resident_pages.shape[1]
+    new_count = new_slots.shape[0]
     bf16 = jnp.bfloat16
     dma = pltpu.SemaphoreType.DMA
-    return pl.pallas_call(
+    half_keys = pages // new_count * page_size // 2
+    rows = (new_count, page_size // 2, HD)
+    partial = pl.pallas_call(
         exchange_kernel,
         name="exchange_and_attend",
         out_shape=(
-            jax.ShapeDtypeStruct(queries.shape, queries.dtype),
             jax.ShapeDtypeStruct((pages,) + resident_pages.shape[1:], bf16),
+            jax.ShapeDtypeStruct(block_table.shape[:1] + queries.shape[1:], bf16),
+            jax.ShapeDtypeStruct((new_count, 2, page_size // 2, half_keys), bf16),
+            jax.ShapeDtypeStruct(rows, jnp.float32),
+            jax.ShapeDtypeStruct(rows, jnp.float32),
         ),
         in_specs=[ANY] * 10,
-        out_specs=(VMEM, VMEM),
+        out_specs=(VMEM,) * 5,
         scratch_shapes=[
             pltpu.VMEM(queries.shape, bf16),
             pltpu.VMEM(new_kv.shape, bf16),
@@ -433,7 +506,6 @@
             pltpu.VMEM((page_size // 2, HD), jnp.float32),
             pltpu.VMEM((16, 2 * HD), jnp.float32),
             pltpu.VMEM((page_size // 2, HD), jnp.float32),
-            pltpu.VMEM(queries.shape, jnp.float32),
             dma((10,)),
             dma((2,)),
             dma((6,)),
@@ -460,6 +532,23 @@
         )
     )
 
+    return pl.pallas_call(
+        finish_kernel,
+        name="finish_fresh",
+        out_shape=(
+            jax.ShapeDtypeStruct(queries.shape, bf16),
+            jax.ShapeDtypeStruct((pages,) + resident_pages.shape[1:], bf16),
+        ),
+        in_specs=[VMEM] * 5 + [ANY],
+        out_specs=(VMEM, ANY),
+        scratch_shapes=[
+            pltpu.SMEM(new_slots.shape, jnp.int32),
+            pltpu.VMEM((page_size // 2, HD), jnp.float32),
+            dma((2,)),
+        ],
+        compiler_params=pltpu.CompilerParams(vmem_limit_bytes=16 << 20),
+    )(*partial, pltpu.with_memory_space_constraint(new_slots, pltpu.HBM))
+
 
 def solution(mesh):
     return jax.shard_map(

time: 46.5 us -> 44.1 us (0.948); the launches traced: 45.9 us -> 44 us
  local copies, waits for them, and re-layouts: 1.58 us -> 0 us
    pallas_call x1, Pallas kernels: 43.6 us -> 41.7 us  [on_device(): pl.pallas_call(exchange_kernel, name='exchange_and_attend', out_shape=(ja...]
    pallas_call x0 -> x1, Pallas kernels: none -> 1.6 us  [on_device(): pl.pallas_call(finish_kernel, name='finish_fresh', out_shape=(jax.ShapeDt...]
    unnamed x2 -> x0, local copies, waits for them, and re-layouts: 1.58 us -> none
where the time goes in v3:
time: 44.1 us; the launch traced here: 44 us
  Pallas kernels  43.3 us (98%)
  between operations  0.64 us (1%)
    pallas_call x1, Pallas kernels, on_device(): pl.pallas_call(exchange_kernel, name='exchange_and_attend', out_shape=(ja...  41.7 us
    pallas_call x1, Pallas kernels, on_device(): pl.pallas_call(finish_kernel, name='finish_fresh', out_shape=(jax.ShapeDt...  1.6 us

profile of v3, /device:TPU:7, one launch (start us, length us, event | category | flops | bytes accessed | tf_op | source)
XLA Modules:
  0.0 44.0 jit_solution(1460124893742512723)
XLA Ops:
  0.6 41.7 %exchange_and_attend.1 = (bf16[28,64,256]{2,1,0:T(8,128)(2,1)S(1)}, bf16[12,4,1024]{2,1,0:T(4,128)(2,1)S(1)}, bf16[4,2,32,224]{3,2,1,0:T(8,128)(2,1)S(1)}, f32[4,32,128]{2,1,0:T(8,128)S(1)}, f32[4,32,128]{2,1,0:T(8,128)S(1)}) custom-call(bf16[16,4,1024]{2,1,0:T(4,128)(2,1)} %queries.1, bf16[16,4,256]{2,1,0:T(4,128)(2,1)} %new_kv.1, ...), custom_call_target="tpu_custom_call" | custom-call | tf_op jit(solution)/shard_map/exchange_and_attend/pallas_call | solution.py:472
  42.4 1.6 %finish_fresh.1 = (bf16[16,4,1024]{2,1,0:T(4,128)(2,1)}, bf16[28,64,256]{2,1,0:T(8,128)(2,1)}) custom-call(bf16[28,64,256]{2,1,0:T(8,128)(2,1)S(1)} %get-tuple-element.7.arrived, bf16[12,4,1024]{2,1,0:T(4,128)(2,1)S(1)} %get-tuple-element.8.results, bf16[4,2,32,224]{3,2,1,0:T(8,128)(2,1)S(1)} %get-tuple-element.9.fresh_weights, ...), custom_call_target="tpu_custom_call" | custom-call | tf_op jit(solution)/shard_map/finish_fresh/pallas_call | solution.py:535

commit v4 on v3

--- a/solution.py
+++ b/solution.py
@@ -44,6 +44,7 @@
     arrived_out,
     slots_s,
     rows_v,
+    attention_v,
     sems,
 ):
     slots_copy = pltpu.make_async_copy(new_slots, slots_s, sems.at[0])
@@ -55,21 +56,26 @@
     others = pl.ds(pl.multiple_of(other * part, part), part)
     new_count = fresh_sums.shape[0]
     pages_each = arrived.shape[0] // new_count
-    slots_copy.wait()
-    for m in range(results.shape[0]):
-        slot = m
-        for k in range(new_count):
-            slot = slot + jnp.where(slots_s[k] <= slot, 1, 0)
-        attention_out[slot] = results[m]
+    fresh = []
     for k in range(new_count):
         first_page = k * pages_each
         values = jnp.concatenate(
             [arrived[first_page + j, others, HD:] for j in range(pages_each)], axis=0
         )
         rows = jnp.dot(fresh_weights[k, other], values, preferred_element_type=jnp.float32)
-        rows = (fresh_sums[k] + rows) / denominators[k]
-        split_rows(rows, rows_v, attention_out, slots_s[k])
+        fresh.append((fresh_sums[k] + rows) / denominators[k])
+    slots_copy.wait()
+    for m in range(results.shape[0]):
+        slot = m
+        for k in range(new_count):
+            slot = slot + jnp.where(slots_s[k] <= slot, 1, 0)
+        attention_v[slot] = results[m]
+    for k in range(new_count):
+        split_rows(fresh[k], rows_v, attention_v, slots_s[k])
+    out = pltpu.make_async_copy(attention_v, attention_out, sems.at[2])
+    out.start()
     copy.wait()
+    out.wait()
 
 
 def exchange_kernel(
@@ -148,14 +154,22 @@
 
     barrier = pltpu.get_barrier_semaphore()
 
+    x0 = me // 8
+    z0 = me % 8
+    mine_at = jnp.where(x0 < 2, me, 16 + z0 % 4 * 4 + z0 // 4 * 2 + x0 % 2)
+
     def peer(k):
-        return jnp.where(k < me, k, k + 1)
-
-    def greet_group(k, carry):
-        pl.semaphore_signal(barrier, inc=1, device_id=(peer(k), place), device_id_type=MESH)
-        return carry
-
-    lax.fori_loop(0, groups - 1, greet_group, 0)
+        at = jnp.where(k < mine_at, k, k + 1)
+        i = at % 16
+        return jnp.where(at < 16, at, (2 + i % 2) * 8 + i // 4 + i // 2 % 2 * 4)
+
+    for dz in (4, 3, 5, 2, 6, 1, 7, 0):
+        for dx in (2, 1, 3, 0):
+            if dx or dz:
+                other = (me // 8 + dx) % 4 * 8 + (me + dz) % 8
+                pl.semaphore_signal(
+                    barrier, inc=1, device_id=(other, place), device_id_type=MESH
+                )
 
     def greet_place(k, carry):
         other = core * chips + k
@@ -166,7 +180,7 @@
 
         return carry
 
-    lax.fori_loop(0, chips, greet_place, 0)
+    lax.fori_loop(0, chips, greet_place, 0, unroll=True)
     sibling = chip * 2 + 1 - core
     pl.semaphore_signal(barrier, inc=1, device_id=(me, sibling), device_id_type=MESH)
     start(loads[2:])
@@ -265,15 +279,33 @@
         def _():
             pltpu.make_async_copy(target.at[0], target.at[0], send_sems.at[n]).wait()
 
-    to_groups(key_send, key_recv, 0)
     to_chips(
         lambda h: arriving_v.at[:, :, pl.ds(pl.multiple_of((2 * h + 1) * HD, HD), HD)],
         value_rows,
         1,
     )
-
-    wait(loads[4:])
-
+    to_groups(key_send, key_recv, 0)
+
+    wait(loads[2:])
+
+    def pick(b, carry):
+        chosen, counts = carry
+        seen = 0
+        for i in range(pages):
+            j = b * pages + i
+            mine = owner_s[j] == me
+            hit = lane == jnp.where(mine, position_s[j], -1)
+            chosen = jnp.where(hit, 2 * b + seen, chosen)
+            counts = jnp.where(hit, tokens_s[j], counts)
+            seen = jnp.where(mine, 1, seen)
+        return chosen, counts
+
+    zero = jnp.zeros((8, 128), jnp.int32)
+    chosen, counts = lax.fori_loop(0, groups, pick, (zero, zero))
+    pick_v[...] = jnp.where(row == 0, chosen, counts)
+    copy = pltpu.make_async_copy(pick_v, pick_s, table_sems.at[1])
+    copy.start()
+    copy.wait()
     fresh_rows[...] = jnp.zeros_like(fresh_rows)
     factor = 1.0 / math.sqrt(HD)
 
@@ -320,7 +352,7 @@
         store_result(m, weigh(weights, cache[:, HD:]) / denominator)
         return carry
 
-    lax.fori_loop(0, 3, resident, 0)
+    lax.fori_loop(0, 5, resident, 0)
 
     chips_arrived(value_rows, 1)
 
@@ -333,28 +365,7 @@
     lax.fori_loop(0, groups, pack_values, 0, unroll=2)
     to_groups(value_send, value_recv, 2)
 
-    loads[2].wait()
-    loads[3].wait()
-
-    def pick(b, carry):
-        chosen, counts = carry
-        seen = 0
-        for i in range(pages):
-            j = b * pages + i
-            mine = owner_s[j] == me
-            hit = lane == jnp.where(mine, position_s[j], -1)
-            chosen = jnp.where(hit, 2 * b + seen, chosen)
-            counts = jnp.where(hit, tokens_s[j], counts)
-            seen = jnp.where(mine, 1, seen)
-        return chosen, counts
-
-    zero = jnp.zeros((8, 128), jnp.int32)
-    chosen, counts = lax.fori_loop(0, groups, pick, (zero, zero))
-    pick_v[...] = jnp.where(row == 0, chosen, counts)
-    copy = pltpu.make_async_copy(pick_v, pick_s, table_sems.at[1])
-    copy.start()
-    copy.wait()
-    lax.fori_loop(3, 7, resident, 0)
+    lax.fori_loop(5, 6, resident, 0)
 
     groups_arrived(key_recv, 0)
 
@@ -368,7 +379,7 @@
     lax.fori_loop(0, pages, turn_keys, 0, unroll=4)
     to_chips(lambda h: key_turn.at[h], key_rows, 3)
 
-    lax.fori_loop(7, old_count, resident, 0)
+    lax.fori_loop(6, old_count, resident, 0)
 
     chips_arrived(key_rows, 3)
     mine = pl.ds(pl.multiple_of(core * part, part), part)
@@ -540,11 +551,12 @@
             jax.ShapeDtypeStruct((pages,) + resident_pages.shape[1:], bf16),
         ),
         in_specs=[VMEM] * 5 + [ANY],
-        out_specs=(VMEM, ANY),
+        out_specs=(ANY, ANY),
         scratch_shapes=[
             pltpu.SMEM(new_slots.shape, jnp.int32),
             pltpu.VMEM((page_size // 2, HD), jnp.float32),
-            dma((2,)),
+            pltpu.VMEM(queries.shape, bf16),
+            dma((3,)),
         ],
         compiler_params=pltpu.CompilerParams(vmem_limit_bytes=16 << 20),
     )(*partial, pltpu.with_memory_space_constraint(new_slots, pltpu.HBM))

time: 44.1 us -> 42.8 us (0.971); the launches traced: 44 us -> 42.2 us
  Pallas kernels: 43.3 us -> 41.5 us
    pallas_call x1, Pallas kernels: 41.7 us -> 40.1 us  [on_device(): pl.pallas_call(exchange_kernel, name='exchange_and_attend', out_shape=(ja...]
where the time goes in v4:
time: 42.8 us; the launch traced here: 42.2 us
  Pallas kernels  41.5 us (97%)
  between operations  0.64 us (1%)
    pallas_call x1, Pallas kernels, on_device(): pl.pallas_call(exchange_kernel, name='exchange_and_attend', out_shape=(ja...  40.1 us
    pallas_call x1, Pallas kernels, on_device(): pl.pallas_call(finish_kernel, name='finish_fresh', out_shape=(jax.ShapeDt...  1.44 us

profile of v4, /device:TPU:7, one launch (start us, length us, event | category | flops | bytes accessed | tf_op | source)
XLA Modules:
  0.0 42.2 jit_solution(11516078056879549683)
XLA Ops:
  0.6 40.1 %exchange_and_attend.1 = (bf16[28,64,256]{2,1,0:T(8,128)(2,1)S(1)}, bf16[12,4,1024]{2,1,0:T(4,128)(2,1)S(1)}, bf16[4,2,32,224]{3,2,1,0:T(8,128)(2,1)S(1)}, f32[4,32,128]{2,1,0:T(8,128)S(1)}, f32[4,32,128]{2,1,0:T(8,128)S(1)}) custom-call(bf16[16,4,1024]{2,1,0:T(4,128)(2,1)} %queries.1, bf16[16,4,256]{2,1,0:T(4,128)(2,1)} %new_kv.1, ...), custom_call_target="tpu_custom_call" | custom-call | tf_op jit(solution)/shard_map/exchange_and_attend/pallas_call | solution.py:483
  40.8 1.4 %finish_fresh.1 = (bf16[16,4,1024]{2,1,0:T(4,128)(2,1)}, bf16[28,64,256]{2,1,0:T(8,128)(2,1)}) custom-call(bf16[28,64,256]{2,1,0:T(8,128)(2,1)S(1)} %get-tuple-element.7.arrived, bf16[12,4,1024]{2,1,0:T(4,128)(2,1)S(1)} %get-tuple-element.8.results, bf16[4,2,32,224]{3,2,1,0:T(8,128)(2,1)S(1)} %get-tuple-element.9.fresh_weights, ...), custom_call_target="tpu_custom_call" | custom-call | tf_op jit(solution)/shard_map/finish_fresh/pallas_call | solution.py:546

commit v5 on v4

--- a/solution.py
+++ b/solution.py
@@ -14,6 +14,8 @@
 MESH = pl.DeviceIdType.MESH
 ANY = pl.BlockSpec(memory_space=pl.ANY)
 VMEM = pl.BlockSpec(memory_space=pltpu.VMEM)
+
+GROUP_ORDER = [*range(16)] + [x * 8 + z for z in (0, 1, 4, 2, 5, 3, 6, 7) for x in (2, 3)]
 
 
 def start(copies):
@@ -44,6 +46,7 @@
     arrived_out,
     slots_s,
     rows_v,
+    fresh_v,
     attention_v,
     sems,
 ):
@@ -56,14 +59,13 @@
     others = pl.ds(pl.multiple_of(other * part, part), part)
     new_count = fresh_sums.shape[0]
     pages_each = arrived.shape[0] // new_count
-    fresh = []
     for k in range(new_count):
         first_page = k * pages_each
         values = jnp.concatenate(
             [arrived[first_page + j, others, HD:] for j in range(pages_each)], axis=0
         )
         rows = jnp.dot(fresh_weights[k, other], values, preferred_element_type=jnp.float32)
-        fresh.append((fresh_sums[k] + rows) / denominators[k])
+        split_rows((fresh_sums[k] + rows) / denominators[k], rows_v, fresh_v, k)
     slots_copy.wait()
     for m in range(results.shape[0]):
         slot = m
@@ -71,7 +73,7 @@
             slot = slot + jnp.where(slots_s[k] <= slot, 1, 0)
         attention_v[slot] = results[m]
     for k in range(new_count):
-        split_rows(fresh[k], rows_v, attention_v, slots_s[k])
+        attention_v[slots_s[k]] = fresh_v[k]
     out = pltpu.make_async_copy(attention_v, attention_out, sems.at[2])
     out.start()
     copy.wait()
@@ -154,15 +156,6 @@
 
     barrier = pltpu.get_barrier_semaphore()
 
-    x0 = me // 8
-    z0 = me % 8
-    mine_at = jnp.where(x0 < 2, me, 16 + z0 % 4 * 4 + z0 // 4 * 2 + x0 % 2)
-
-    def peer(k):
-        at = jnp.where(k < mine_at, k, k + 1)
-        i = at % 16
-        return jnp.where(at < 16, at, (2 + i % 2) * 8 + i // 4 + i // 2 % 2 * 4)
-
     for dz in (4, 3, 5, 2, 6, 1, 7, 0):
         for dx in (2, 1, 3, 0):
             if dx or dz:
@@ -215,19 +208,18 @@
         own = pltpu.make_async_copy(source.at[me], target.at[me], recv_sems.at[n])
         own.start()
 
-        def send(k, carry):
-            other = peer(k)
-            pltpu.make_async_remote_copy(
-                src_ref=source.at[other],
-                dst_ref=target.at[me],
-                send_sem=send_sems.at[n],
-                recv_sem=recv_sems.at[n],
-                device_id=(other, place),
-                device_id_type=MESH,
-            ).start()
-            return carry
-
-        lax.fori_loop(0, groups - 1, send, 0)
+        for other in GROUP_ORDER:
+
+            @pl.when(me != other)
+            def _():
+                pltpu.make_async_remote_copy(
+                    src_ref=source.at[other],
+                    dst_ref=target.at[me],
+                    send_sem=send_sems.at[n],
+                    recv_sem=recv_sems.at[n],
+                    device_id=(other, place),
+                    device_id_type=MESH,
+                ).start()
 
     def groups_arrived(target, n):
         pltpu.make_async_copy(target, target, recv_sems.at[n]).wait()
@@ -555,6 +547,7 @@
         scratch_shapes=[
             pltpu.SMEM(new_slots.shape, jnp.int32),
             pltpu.VMEM((page_size // 2, HD), jnp.float32),
+            pltpu.VMEM((new_count,) + queries.shape[1:], bf16),
             pltpu.VMEM(queries.shape, bf16),
             dma((3,)),
         ],

time: 42.8 us -> 42.6 us (level)
  no operation moved by 1% of the time
where the time goes in v5:
time: 42.6 us; the launch traced here: 42.2 us
  Pallas kernels  41.6 us (98%)
  between operations  0.64 us (2%)
    pallas_call x1, Pallas kernels, on_device(): pl.pallas_call(exchange_kernel, name='exchange_and_attend', out_shape=(ja...  40.2 us
    pallas_call x1, Pallas kernels, on_device(): pl.pallas_call(finish_kernel, name='finish_fresh', out_shape=(jax.ShapeDt...  1.43 us

profile of v5, /device:TPU:7, one launch (start us, length us, event | category | flops | bytes accessed | tf_op | source)
XLA Modules:
  0.0 42.2 jit_solution(9493991339339975811)
XLA Ops:
  0.6 40.2 %exchange_and_attend.1 = (bf16[28,64,256]{2,1,0:T(8,128)(2,1)S(1)}, bf16[12,4,1024]{2,1,0:T(4,128)(2,1)S(1)}, bf16[4,2,32,224]{3,2,1,0:T(8,128)(2,1)S(1)}, f32[4,32,128]{2,1,0:T(8,128)S(1)}, f32[4,32,128]{2,1,0:T(8,128)S(1)}) custom-call(bf16[16,4,1024]{2,1,0:T(4,128)(2,1)} %queries.1, bf16[16,4,256]{2,1,0:T(4,128)(2,1)} %new_kv.1, ...), custom_call_target="tpu_custom_call" | custom-call | tf_op jit(solution)/shard_map/exchange_and_attend/pallas_call | solution.py:475
  40.8 1.4 %finish_fresh.1 = (bf16[16,4,1024]{2,1,0:T(4,128)(2,1)}, bf16[28,64,256]{2,1,0:T(8,128)(2,1)}) custom-call(bf16[28,64,256]{2,1,0:T(8,128)(2,1)S(1)} %get-tuple-element.7.arrived, bf16[12,4,1024]{2,1,0:T(4,128)(2,1)S(1)} %get-tuple-element.8.results, bf16[4,2,32,224]{3,2,1,0:T(8,128)(2,1)S(1)} %get-tuple-element.9.fresh_weights, ...), custom_call_target="tpu_custom_call" | custom-call | tf_op jit(solution)/shard_map/finish_fresh/pallas_call | solution.py:538
